TPU v7x, 512 devices: a whole 4x8x8 slice. The times are simulated.
512 devices in a mesh: dp: 8 (over x, core), tensor: 8 (over z), vocab: 8 (over y).
Axes of the slice: x: 4, y: 8, z: 8, core: 2. Of those that a mesh axis runs over, the one named last changes fastest.
Arguments:
- hidden_in: bfloat16 [1024, 4608], P('dp')
- norm_pre: float32 [4608], replicated, may hold values from 0.1 to 1.9
- w_gate: bfloat16 [4608, 18432], P('dp', ('tensor', 'vocab')), may hold values from -0.09375 to 0.09375
- w_up: bfloat16 [4608, 18432], P('dp', ('tensor', 'vocab')), may hold values from -0.09375 to 0.09375
- w_down: bfloat16 [18432, 4608], P(('tensor', 'vocab'), 'dp'), may hold values from -0.125 to 0.125
- norm_post: float32 [4608], replicated, may hold values from 0.1 to 1.9
- norm_final: float32 [4608], replicated, may hold values from 0.1 to 1.9
- unembed: bfloat16 [4608, 131072], P(None, ('dp', 'tensor', 'vocab')), may hold values from -0.375 to 0.375
- token_ids: int32 [1024], P('dp'), may hold values from 0 to 131071
- lengths: int32 [16], P('dp'), may hold values from 1 to 63, as said below
Outputs:
- token_logprob: float32 [1024], P('dp')
Inputs may be any that keep to these rules, and one draw needn't show every extreme that they name: The rollouts are numbered by index of dp, 2 to each; the lengths of the rollouts of one index of dp sum to at most 64, and to exactly 64 on at least one index of dp, whose rollouts have lengths 64 - 1 and 1.
All inputs are finite; a program needn't handle non-finite values.
Results may differ from a plain program's by a relative error of at most 0.0035.
Values may be sent and summed in bfloat16 or wider, within the bound.
A program may use at most 64 MiB of HBM per device.

v0:
```python
import jax
import jax.numpy as jnp
from jax import lax
from jax.sharding import PartitionSpec as P

EPS = 1e-06
CAP = 30.0


def on_device(
    hidden_in, norm_pre, w_gate, w_up, w_down, norm_post, norm_final, unembed, token_ids, lengths
):
    slot_count = hidden_in.shape[0]
    segment = slot_count // lengths.shape[0]
    position = jnp.arange(slot_count, dtype=jnp.int32)
    which = (position // segment)[:, None] == jnp.arange(lengths.shape[0], dtype=jnp.int32)[None, :]
    bounds = jnp.sum(jnp.where(which, lengths[None, :], 0), axis=1)
    scored = position % segment < bounds
    stream_in = hidden_in.astype(jnp.float32)
    normed = (
        stream_in
        * lax.rsqrt(jnp.mean(stream_in * stream_in, axis=1, keepdims=True) + EPS)
        * norm_pre
    ).astype(jnp.bfloat16)
    spread = lax.all_to_all(normed, "dp", split_axis=1, concat_axis=0, tiled=True)
    paired = jnp.concatenate([w_gate, w_up], axis=1)
    gate_up = lax.psum_scatter(
        jnp.dot(spread, paired, preferred_element_type=jnp.float32).astype(jnp.bfloat16),
        "dp",
        scatter_dimension=0,
        tiled=True,
    ).astype(jnp.float32)
    units = w_gate.shape[1]
    hidden = (jax.nn.silu(gate_up[:, :units]) * gate_up[:, units:]).astype(jnp.bfloat16)
    branch = jnp.dot(
        hidden, lax.all_gather(w_down, "dp", axis=1, tiled=True), preferred_element_type=jnp.float32
    )
    summed = lax.psum(branch, ("tensor", "vocab"))
    stream = (
        stream_in
        + summed * lax.rsqrt(jnp.mean(summed * summed, axis=1, keepdims=True) + EPS) * norm_post
    )
    final = (
        stream * lax.rsqrt(jnp.mean(stream * stream, axis=1, keepdims=True) + EPS) * norm_final
    ).astype(jnp.bfloat16)
    every_row, every_target = (
        lax.all_gather(final, "dp", axis=0, tiled=True),
        lax.all_gather(token_ids, "dp", axis=0, tiled=True),
    )
    shard = unembed.shape[1]
    offset = lax.axis_index(("dp", "tensor", "vocab")) * shard
    capped = CAP * jnp.tanh(jnp.dot(every_row, unembed, preferred_element_type=jnp.float32) / CAP)
    totals = jnp.sum(jnp.exp(capped - CAP), axis=1)
    matches = jnp.arange(shard, dtype=jnp.int32)[None, :] + offset == every_target[:, None]
    sampled = jnp.sum(jnp.where(matches, capped, 0.0), axis=1)
    every_total, every_sampled = lax.psum((totals, sampled), ("dp", "tensor", "vocab"))
    count = every_total.shape[0] // lax.axis_size("dp")
    start = lax.axis_index("dp") * count
    own_total = lax.dynamic_slice_in_dim(every_total, start, count, 0)
    own_target = lax.dynamic_slice_in_dim(every_sampled, start, count, 0)
    logprob = own_target - CAP - jnp.log(own_total)
    return jnp.where(scored, logprob, 0.0)


def solution(mesh):
    in_specs = (
        P("dp", None),
        P(),
        P("dp", ("tensor", "vocab")),
        P("dp", ("tensor", "vocab")),
        P(("tensor", "vocab"), "dp"),
        P(),
        P(),
        P(None, ("dp", "tensor", "vocab")),
        P("dp"),
        P("dp"),
    )
    out_specs = P("dp")
    return jax.shard_map(
        on_device, mesh=mesh, in_specs=in_specs, out_specs=out_specs, check_vma=False
    )
```

profile of v0, /device:TPU:1, one launch (start us, length us, event | category | flops | bytes accessed | tf_op | source)
XLA Modules:
  0.0 464.3 jit_solution(11924387753720224544)
XLA Ops:
  6.5 1.7 fusion
  8.3 2.6 fusion.2
  10.9 1.7 copy.17
  12.6 26.1 %all_to_all.19 = bf16[128,8,576]{0,2,1:T(8,128)(2,1)S(1)} all-to-all(bf16[128,8,576]{0,2,1:T(8,128)(2,1)S(1)} %bitcast.20), channel_id=1, replica_groups=mesh['dp'=8,'tensor'=8,'vocab'=8] {'dp'}, dimensions={1} | all-to-all | bytes 2359296 | tf_op jit(solution)/shard_map/all_to_all | solution.py:25
  38.7 1.1 convolution_convert_fusion
  39.8 1.4 copy.20
  41.3 0.7 all-gather.7.cloned.1.call-update
  42.1 34.6 %reduce-scatter.4.cloned.1.call-done = bf16[128,576]{1,0:T(8,128)(2,1)} async-done(((bf16[1024,576]{1,0:T(8,128)(2,1)}), bf16[128,576]{1,0:T(8,128)(2,1)}) %reduce-scatter.4.cloned.1.call-update) | async-done | bytes 147472
  76.6 1.1 copy.21
  77.7 34.4 %all-gather.7.cloned.1.call-done = bf16[8,576,288]{1,2,0:T(8,128)(2,1)} async-done(((bf16[1,576,288]{1,2,0:T(8,128)(2,1)}), bf16[8,576,288]{1,2,0:T(8,128)(2,1)}) %all-gather.7.cloned.1.call-update) | async-done | bytes 2654224 | tf_op jit(solution)/shard_map/all_gather | solution.py:36
  112.1 4.5 copy.19
  116.5 5.6 %reshape.53 = bf16[4608,288]{0,1:T(8,128)(2,1)} reshape(bf16[8,576,288]{1,0,2:T(8,128)(2,1)} %copy.19) | data formatting | bytes 5308416
  122.1 4.0 fusion.11
  126.2 160.6 %all-reduce.3.cloned.1.call-done = f32[128,4608]{1,0:T(8,128)} async-done(((f32[128,4608]{1,0:T(8,128)}), f32[128,4608]{1,0:T(8,128)}) %all-reduce.3.cloned.1.call-update) | async-done | bytes 2359312 | tf_op jit(solution)/shard_map/psum | solution.py:38
  286.8 2.1 multiply_reduce_fusion.1
  288.9 0.3 copy-done.1
  289.2 1.4 multiply_reduce_fusion
  290.6 1.6 multiply_convert_fusion
  292.3 14.7 %all-gather = s32[8,1,128]{2,1,0:T(1,128)S(1)} all-gather(s32[1,1,128]{2,1,0:T(1,128)S(1)} %bitcast.23), channel_id=1, replica_groups=mesh['dp'=8,'tensor'=8,'vocab'=8] {'dp'}, dimensions={0}, use_global_device_ids=true | all-gather | bytes 4608 | tf_op jit(solution)/shard_map/all_gather | solution.py:48
  307.0 0.1 fusion.14
  307.0 45.5 %all-gather.5.cloned.1.call-done = bf16[1024,4608]{1,0:T(8,128)(2,1)} async-done(((bf16[128,4608]{1,0:T(8,128)(2,1)}), bf16[1024,4608]{1,0:T(8,128)(2,1)}) %all-gather.5.cloned.1.call-update) | async-done | bytes 9437200 | tf_op jit(solution)/shard_map/all_gather | solution.py:47
  352.5 6.6 %select_reduce_fusion = (f32[1024]{0:T(1024)S(1)}, f32[1024]{0:T(1024)S(1)}) fusion(s32[1024]{0:T(1024)S(1)} %bitcast.22, s32[256]{0:T(256)S(1)} %iota_add_fusion, bf16[1024,4608]{1,0:T(8,128)(2,1)} %all-gather.5.cloned.1.call-done, bf16[4608,256]{1,0:T(8,128)(2,1)S(1)} %copy-done), kind=kOutput, calls=%fused_computation.16 | convolution fusion | flops 2417752064 | bytes 11809792 | tf_op jit(solution)/shard_map/dot_general | solution.py:52
  359.1 98.1 %all-reduce = (f32[1024]{0:T(1024)S(1)}, f32[1024]{0:T(1024)S(1)}) all-reduce(f32[1024]{0:T(1024)S(1)} %get-tuple-element.6, f32[1024]{0:T(1024)S(1)} %get-tuple-element.5), channel_id=1, replica_groups=mesh['dp'=8,'tensor'=8,'vocab'=8] {'dp','tensor','vocab'}, use_global_device_ids=true, to_apply=%region_9.10 | all-reduce | flops 2048 | bytes 16384 | tf_op jit(solution)/shard_map/psum | solution.py:56
  457.2 0.6 compare_select_fusion
  (30 shorter events, 0.3 us)
Async XLA Ops:
  6.5 346.0 %copy-start = (bf16[4608,256]{1,0:T(8,128)(2,1)S(1)}, bf16[4608,256]{1,0:T(8,128)(2,1)}, u32[]{:S(2)}) copy-start(bf16[4608,256]{1,0:T(8,128)(2,1)} %param.17) | copy-start | bytes 7077892
  6.5 70.1 %reduce-scatter.4.cloned.1.call-start = ((), (), s32[]{:S(2)}) async-start(), calls=%async_computation.5 | async-start | bytes 1474560
  12.6 26.1 %copy-start.6 = (bf16[576,288]{0,1:T(8,128)(2,1)S(1)}, bf16[576,288]{0,1:T(8,128)(2,1)}, u32[]{:S(2)}) copy-start(bf16[576,288]{0,1:T(8,128)(2,1)} %param.13) | copy-start | bytes 995332
  12.6 26.1 %copy-start.7 = (bf16[576,288]{0,1:T(8,128)(2,1)S(1)}, bf16[576,288]{0,1:T(8,128)(2,1)}, u32[]{:S(2)}) copy-start(bf16[576,288]{0,1:T(8,128)(2,1)} %param.12) | copy-start | bytes 995332
  41.3 70.8 %all-gather.7.cloned.1.call-start = ((), (), s32[]{:S(2)}) async-start(), calls=%async_computation.4 | async-start | bytes 3317760 | tf_op jit(solution)/shard_map/all_gather | solution.py:36
  42.0 244.8 %all-reduce.3.cloned.1.call-start = ((), (), s32[]{:S(2)}) async-start(), calls=%async_computation.2 | async-start | bytes 4718592 | tf_op jit(solution)/shard_map/psum | solution.py:38
  126.1 162.8 %copy-start.2 = (bf16[128,4608]{1,0:T(8,128)(2,1)S(1)}, bf16[128,4608]{1,0:T(8,128)(2,1)}, u32[]{:S(2)}) copy-start(bf16[128,4608]{1,0:T(8,128)(2,1)} %param.10) | copy-start | bytes 3538948
  126.1 226.4 %all-gather.5.cloned.1.call-start = ((), (), s32[]{:S(2)}) async-start(), calls=%async_computation.3 | async-start | bytes 10616832 | tf_op jit(solution)/shard_map/all_gather | solution.py:47
  286.8 2.4 copy-start.1
  288.9 1.7 copy-start.3
  288.9 1.7 copy-start.4
  290.6 1.7 copy-start.5
  290.6 16.4 %copy-start.8 = (s32[2]{0:T(128)S(1)}, s32[2]{0:T(128)}, u32[]{:S(2)}) copy-start(s32[2]{0:T(128)} %param.19) | copy-start | bytes 28
Sparse Core Ops, SparseCore 0:
  41.4 35.1 reduce-scatter.3
  78.7 33.2 all-gather.6
  126.3 160.4 all-reduce.2
  292.4 60.1 all-gather.4
where the time goes:
time: 465 us; the launch traced here: 464 us
  waiting for transfers between devices  276 us (59%)
  blocking collectives  139 us (30%)
  local copies, waits for them, and re-layouts  14.6 us (3%)
  between operations  13.3 us (3%)
  matrix products  11.7 us (3%)
  other arithmetic  10.1 us (2%)
    psum x1, waiting for transfers between devices, on_device(): summed = lax.psum(branch, ('tensor', 'vocab'))  161 us
    psum x1, blocking collectives, on_device(): lax.psum((totals, sampled), ('dp', 'tensor', 'vocab'))  98.1 us
    all_gather x1, waiting for transfers between devices, on_device(): lax.all_gather(final, 'dp', axis=0, tiled=True)  45.5 us
    unnamed x5, waiting for transfers between devices  35.3 us
    all_gather x1, waiting for transfers between devices, on_device(): lax.all_gather(w_down, 'dp', axis=1, tiled=True)  34.4 us
    all_to_all x1, blocking collectives, on_device(): lax.all_to_all(normed, 'dp', split_axis=1, concat_axis=0, tiled=True)  26.1 us
    all_gather x1, blocking collectives, on_device(): lax.all_gather(token_ids, 'dp', axis=0, tiled=True)  14.7 us
  transfers between devices with their start and end apart: 4, of which 4 were waited for; matrix products, arithmetic and copies ran while one was open for 0% of the time, Pallas kernels for 0%

commit v1 on v0

--- a/solution.py
+++ b/solution.py
@@ -5,6 +5,28 @@
 
 EPS = 1e-06
 CAP = 30.0
+
+
+def laid_out(parts, dim):
+    parts = jnp.moveaxis(parts, 0, dim)
+    lengths = parts.shape
+    return parts.reshape(*lengths[:dim], lengths[dim] * lengths[dim + 1], *lengths[dim + 2 :])
+
+
+def gather_around(array, axis, dim):
+    peers = lax.axis_size(axis)
+    pairs = [(i, (i + 1) % peers) for i in range(peers)]
+    back = [(b, a) for a, b in pairs]
+    lower, upper = ([], [])
+    for turn in range(peers - 1):
+        if turn % 2 == 0:
+            lower.append(lax.ppermute(lower[-1] if lower else array, axis, pairs))
+        else:
+            upper.append(lax.ppermute(upper[-1] if upper else array, axis, back))
+    pieces = jnp.stack([*lower[::-1], array, *upper])
+    shift = lax.axis_index(axis) - len(lower)
+    pieces = pieces[(jnp.arange(peers) - shift) % peers]
+    return laid_out(pieces, dim)
 
 
 def on_device(
@@ -32,9 +54,7 @@
     ).astype(jnp.float32)
     units = w_gate.shape[1]
     hidden = (jax.nn.silu(gate_up[:, :units]) * gate_up[:, units:]).astype(jnp.bfloat16)
-    branch = jnp.dot(
-        hidden, lax.all_gather(w_down, "dp", axis=1, tiled=True), preferred_element_type=jnp.float32
-    )
+    branch = jnp.dot(hidden, gather_around(w_down, "dp", 1), preferred_element_type=jnp.float32)
     summed = lax.psum(branch, ("tensor", "vocab"))
     stream = (
         stream_in

time: 465 us -> 437 us (0.940)
  waiting for transfers between devices: 276 us -> 233 us
  blocking collectives: 139 us -> 113 us
  starting transfers between devices: 0.12 us -> 24.3 us
  local copies, waits for them, and re-layouts: 14.6 us -> 29.9 us
    all_gather x1 -> x0, waiting for transfers between devices: 34.4 us -> none  [on_device(): lax.all_gather(w_down, 'dp', axis=1, tiled=True)]
    unnamed x5 -> x4, waiting for transfers between devices: 35.3 us -> 3.01 us
    all_to_all x1 -> x0, blocking collectives: 26.1 us -> none  [on_device(): lax.all_to_all(normed, 'dp', split_axis=1, concat_axis=0, tiled=True)]
    ppermute x0 -> x7, waiting for transfers between devices: none -> 23.7 us  [the longest x4 19 us: gather_around(): lower.append(lax.ppermute(lower[-1] if lower else array, axis, pairs))]
    ppermute x0 -> x7, starting transfers between devices: none -> 13.9 us  [the longest x3 7.31 us: gather_around(): upper.append(lax.ppermute(upper[-1] if upper else array, axis, back))]
    all_to_all x0 -> x1, starting transfers between devices: none -> 10.3 us  [on_device(): lax.all_to_all(normed, 'dp', split_axis=1, concat_axis=0, tiled=True)]
    reshape x0 -> x1, local copies, waits for them, and re-layouts: none -> 5.63 us  [laid_out(): parts.reshape(*lengths[:dim], lengths[dim] * lengths[dim + 1], *lengths[d...]
    unnamed x21 -> x29, local copies, waits for them, and re-layouts: 8.42 us -> 13.2 us
  transfers between devices with their start and end apart: 4 -> 11, of which waited for: 4 -> 6; matrix products, arithmetic and copies ran while one was open for 0% -> 7% of each run, Pallas kernels for 0% -> 0%
where the time goes in v1:
time: 437 us; the launch traced here: 436 us
  waiting for transfers between devices  233 us (53%)
  blocking collectives  113 us (26%)
  local copies, waits for them, and re-layouts  29.9 us (7%)
  starting transfers between devices  24.3 us (6%)
  matrix products  13.8 us (3%)
  between operations  13.2 us (3%)
  other arithmetic  9.15 us (2%)
    psum x1, waiting for transfers between devices, on_device(): summed = lax.psum(branch, ('tensor', 'vocab'))  161 us
    psum x1, blocking collectives, on_device(): lax.psum((totals, sampled), ('dp', 'tensor', 'vocab'))  98.1 us
    all_gather x1, waiting for transfers between devices, on_device(): lax.all_gather(final, 'dp', axis=0, tiled=True)  45.5 us
    ppermute x4, waiting for transfers between devices, gather_around(): lower.append(lax.ppermute(lower[-1] if lower else array, axis, pairs))  19 us
    all_gather x1, blocking collectives, on_device(): lax.all_gather(token_ids, 'dp', axis=0, tiled=True)  14.7 us
    unnamed x29, local copies, waits for them, and re-layouts  13.2 us
    all_to_all x1, starting transfers between devices, on_device(): lax.all_to_all(normed, 'dp', split_axis=1, concat_axis=0, tiled=True)  10.3 us
  transfers between devices with their start and end apart: 11, of which 6 were waited for; matrix products, arithmetic and copies ran while one was open for 7% of the time, Pallas kernels for 0%

profile of v1, /device:TPU:1, one launch (start us, length us, event | category | flops | bytes accessed | tf_op | source)
XLA Modules:
  0.0 436.2 jit_solution(18263665475051747251)
XLA Ops:
  11.3 10.3 %all-to-all-start = ((bf16[128,8,576]{0,2,1:T(8,128)(2,1)}), bf16[128,8,576]{0,2,1:T(8,128)(2,1)S(1)}, u32[]{:S(2)}, u32[]{:S(2)}) async-start(bf16[128,8,576]{0,2,1:T(8,128)(2,1)} %bitcast.2), calls=%async_computation | async-start | bytes 2359296 | tf_op jit(solution)/shard_map/all_to_all | solution.py:47
  23.3 15.8 %collective-permute-done = bf16[288,576]{1,0:T(8,128)(2,1)S(1)} collective-permute-done((bf16[288,576]{1,0:T(8,128)(2,1)}, bf16[288,576]{1,0:T(8,128)(2,1)S(1)}, u32[]{:S(2)}, u32[]{:S(2)}) %collective-permute-start) | collective-permute-done | bytes 331808 | tf_op jit(solution)/shard_map/ppermute | solution.py:23
  39.1 2.4 collective-permute-start.1
  42.7 3.2 collective-permute-done.1
  45.9 2.6 collective-permute-start.2
  48.5 3.2 convolution_convert_fusion
  51.7 2.4 copy.20
  54.2 2.5 collective-permute-start.5
  56.7 4.7 %collective-permute-done.5 = bf16[288,576]{1,0:T(8,128)(2,1)S(1)} collective-permute-done((bf16[288,576]{1,0:T(8,128)(2,1)}, bf16[288,576]{1,0:T(8,128)(2,1)S(1)}, u32[]{:S(2)}, u32[]{:S(2)}) %collective-permute-start.5) | collective-permute-done | bytes 331808 | tf_op jit(solution)/shard_map/ppermute | solution.py:25
  61.4 3.6 collective-permute-start.6
  65.0 1.8 bitcast_dynamic-update-slice_fusion.7
  68.5 1.8 bitcast_dynamic-update-slice_fusion.5
  71.9 1.8 bitcast_dynamic-update-slice_fusion.2
  75.2 4.4 %gather_fusion = bf16[8,288,576]{2,1,0:T(8,128)(2,1)} fusion(bf16[8,288,576]{2,1,0:T(8,128)(2,1)} %bitcast_dynamic-update-slice_fusion, s32[1024]{0:T(1024)S(1)} %pad_clamp_fusion), kind=kCustom, calls=%fused_computation | custom fusion | bytes 5308448 | tf_op jit(solution)/shard_map/gather | solution.py:28
  79.6 4.5 %copy.19 = bf16[288,8,576]{2,1,0:T(8,128)(2,1)} copy(bf16[288,8,576]{2,0,1:T(8,128)(2,1)} %bitcast.34) | data formatting | bytes 5308416 | tf_op jit(solution)/shard_map/transpose | solution.py:11
  84.1 5.6 %reshape.102 = bf16[288,4608]{1,0:T(8,128)(2,1)} reshape(bf16[288,8,576]{2,1,0:T(8,128)(2,1)} %copy.19) | data formatting | bytes 5308416 | tf_op jit(solution)/shard_map/reshape | solution.py:13
  89.7 3.0 reduce-scatter.4.cloned.1.call-done
  93.7 4.0 fusion.11
  97.8 161.0 %all-reduce.3.cloned.1.call-done = f32[128,4608]{1,0:T(8,128)} async-done(((f32[128,4608]{1,0:T(8,128)}), f32[128,4608]{1,0:T(8,128)}) %all-reduce.3.cloned.1.call-update) | async-done | bytes 2359312 | tf_op jit(solution)/shard_map/psum | solution.py:58
  258.8 2.1 multiply_reduce_fusion.1
  264.2 14.7 %all-gather = s32[8,1,128]{2,1,0:T(1,128)S(1)} all-gather(s32[1,1,128]{2,1,0:T(1,128)S(1)} %bitcast.36), channel_id=1, replica_groups=mesh['dp'=8,'tensor'=8,'vocab'=8] {'dp'}, dimensions={0}, use_global_device_ids=true | all-gather | bytes 4608 | tf_op jit(solution)/shard_map/all_gather | solution.py:68
  279.0 45.5 %all-gather.3.cloned.1.call-done = bf16[1024,4608]{1,0:T(8,128)(2,1)} async-done(((bf16[128,4608]{1,0:T(8,128)(2,1)}), bf16[1024,4608]{1,0:T(8,128)(2,1)}) %all-gather.3.cloned.1.call-update) | async-done | bytes 9437200 | tf_op jit(solution)/shard_map/all_gather | solution.py:67
  324.5 6.6 %select_reduce_fusion = (f32[1024]{0:T(1024)S(1)}, f32[1024]{0:T(1024)S(1)}) fusion(s32[1024]{0:T(1024)S(1)} %bitcast.35, s32[256]{0:T(256)S(1)} %iota_add_fusion, bf16[1024,4608]{1,0:T(8,128)(2,1)} %all-gather.3.cloned.1.call-done, bf16[4608,256]{1,0:T(8,128)(2,1)S(1)} %copy-done), kind=kOutput, calls=%fused_computation.17 | convolution fusion | flops 2417752064 | bytes 11809792 | tf_op jit(solution)/shard_map/dot_general | solution.py:72
  331.1 98.1 %all-reduce = (f32[1024]{0:T(1024)S(1)}, f32[1024]{0:T(1024)S(1)}) all-reduce(f32[1024]{0:T(1024)S(1)} %get-tuple-element.6, f32[1024]{0:T(1024)S(1)} %get-tuple-element.5), channel_id=1, replica_groups=mesh['dp'=8,'tensor'=8,'vocab'=8] {'dp','tensor','vocab'}, use_global_device_ids=true, to_apply=%region_9.10 | all-reduce | flops 2048 | bytes 16384 | tf_op jit(solution)/shard_map/psum | solution.py:76
  (55 shorter events, 17.8 us)
Async XLA Ops:
  6.5 318.0 %copy-start = (bf16[4608,256]{1,0:T(8,128)(2,1)S(1)}, bf16[4608,256]{1,0:T(8,128)(2,1)}, u32[]{:S(2)}) copy-start(bf16[4608,256]{1,0:T(8,128)(2,1)} %param.17) | copy-start | bytes 7077892
  11.3 37.2 %all-to-all-start = ((bf16[128,8,576]{0,2,1:T(8,128)(2,1)}), bf16[128,8,576]{0,2,1:T(8,128)(2,1)S(1)}, u32[]{:S(2)}, u32[]{:S(2)}) async-start(bf16[128,8,576]{0,2,1:T(8,128)(2,1)} %bitcast.2), calls=%async_computation | async-start | bytes 2359296 | tf_op jit(solution)/shard_map/all_to_all | solution.py:47
  21.7 71.0 %reduce-scatter.4.cloned.1.call-start = ((), (), s32[]{:S(2)}) async-start(), calls=%async_computation.4 | async-start | bytes 1474560
  21.7 17.5 %collective-permute-start = (bf16[288,576]{1,0:T(8,128)(2,1)}, bf16[288,576]{1,0:T(8,128)(2,1)S(1)}, u32[]{:S(2)}, u32[]{:S(2)}) collective-permute-start(bf16[288,576]{1,0:T(8,128)(2,1)} %param.14), channel_id=1, source_target_pairs={{0,64},{64,128},{128,192},{192,256},{256,320},{320,384},{384,448},... | collective-permute-start | bytes 995336 | tf_op jit(solution)/shard_map/ppermute | solution.py:23
  39.1 6.8 %copy-start.4 = (bf16[288,576]{1,0:T(8,128)(2,1)}, bf16[288,576]{1,0:T(8,128)(2,1)S(1)}, u32[]{:S(2)}) copy-start(bf16[288,576]{1,0:T(8,128)(2,1)S(1)} %collective-permute-done) | copy-start | bytes 995332
  39.1 6.8 %collective-permute-start.1 = (bf16[288,576]{1,0:T(8,128)(2,1)S(1)}, bf16[288,576]{1,0:T(8,128)(2,1)}, u32[]{:S(2)}, u32[]{:S(2)}) collective-permute-start(bf16[288,576]{1,0:T(8,128)(2,1)S(1)} %collective-permute-done), channel_id=1, source_target_pairs={{0,64},{64,128},{128,192},{192,256},{256,320},{320,384},{384,448},... | collective-permute-start | bytes 995336 | tf_op jit(solution)/shard_map/ppermute | solution.py:23
  41.5 12.8 %collective-permute-start.4 = (bf16[288,576]{1,0:T(8,128)(2,1)}, bf16[288,576]{1,0:T(8,128)(2,1)}, u32[]{:S(2)}, u32[]{:S(2)}) collective-permute-start(bf16[288,576]{1,0:T(8,128)(2,1)} %param.14), channel_id=1, source_target_pairs={{64,0},{128,64},{192,128},{256,192},{320,256},{384,320},{448,384},... | collective-permute-start | bytes 995336 | tf_op jit(solution)/shard_map/ppermute | solution.py:25
  45.9 10.8 %collective-permute-start.2 = (bf16[288,576]{1,0:T(8,128)(2,1)}, bf16[288,576]{1,0:T(8,128)(2,1)}, u32[]{:S(2)}, u32[]{:S(2)}) collective-permute-start(bf16[288,576]{1,0:T(8,128)(2,1)} %collective-permute-done.1), channel_id=1, source_target_pairs={{0,64},{64,128},{128,192},{192,256},{256,320},{320,384},{384,448},... | collective-permute-start | bytes 995336 | tf_op jit(solution)/shard_map/ppermute | solution.py:23
  54.2 16.1 %copy-start.5 = (bf16[288,576]{1,0:T(8,128)(2,1)S(1)}, bf16[288,576]{1,0:T(8,128)(2,1)}, u32[]{:S(2)}) copy-start(bf16[288,576]{1,0:T(8,128)(2,1)} %copy-done.4) | copy-start | bytes 995332
  54.2 16.9 %copy-start.3 = (bf16[288,576]{1,0:T(8,128)(2,1)S(1)}, bf16[288,576]{1,0:T(8,128)(2,1)}, u32[]{:S(2)}) copy-start(bf16[288,576]{1,0:T(8,128)(2,1)} %param.14) | copy-start | bytes 995332
  54.2 204.6 %all-reduce.3.cloned.1.call-start = ((), (), s32[]{:S(2)}) async-start(), calls=%async_computation.2 | async-start | bytes 4718592 | tf_op jit(solution)/shard_map/psum | solution.py:58
  54.2 7.2 %collective-permute-start.5 = (bf16[288,576]{1,0:T(8,128)(2,1)}, bf16[288,576]{1,0:T(8,128)(2,1)S(1)}, u32[]{:S(2)}, u32[]{:S(2)}) collective-permute-start(bf16[288,576]{1,0:T(8,128)(2,1)} %collective-permute-done.4), channel_id=1, source_target_pairs={{64,0},{128,64},{192,128},{256,192},{320,256},{384,320},{448,384},... | collective-permute-start | bytes 995336 | tf_op jit(solution)/shard_map/ppermute | solution.py:25
  56.7 8.3 %collective-permute-start.3 = (bf16[288,576]{1,0:T(8,128)(2,1)}, bf16[288,576]{1,0:T(8,128)(2,1)}, u32[]{:S(2)}, u32[]{:S(2)}) collective-permute-start(bf16[288,576]{1,0:T(8,128)(2,1)} %collective-permute-done.2), channel_id=1, source_target_pairs={{0,64},{64,128},{128,192},{192,256},{256,320},{320,384},{384,448},... | collective-permute-start | bytes 995336 | tf_op jit(solution)/shard_map/ppermute | solution.py:23
  61.4 13.0 %collective-permute-start.6 = (bf16[288,576]{1,0:T(8,128)(2,1)S(1)}, bf16[288,576]{1,0:T(8,128)(2,1)S(1)}, u32[]{:S(2)}, u32[]{:S(2)}) collective-permute-start(bf16[288,576]{1,0:T(8,128)(2,1)S(1)} %collective-permute-done.5), channel_id=1, source_target_pairs={{64,0},{128,64},{192,128},{256,192},{320,256},{384,320},{448,384},... | collective-permute-start | bytes 995336 | tf_op jit(solution)/shard_map/ppermute | solution.py:25
  97.8 163.1 %copy-start.2 = (bf16[128,4608]{1,0:T(8,128)(2,1)S(1)}, bf16[128,4608]{1,0:T(8,128)(2,1)}, u32[]{:S(2)}) copy-start(bf16[128,4608]{1,0:T(8,128)(2,1)} %param.10) | copy-start | bytes 3538948
  97.8 226.7 %all-gather.3.cloned.1.call-start = ((), (), s32[]{:S(2)}) async-start(), calls=%async_computation.3 | async-start | bytes 10616832 | tf_op jit(solution)/shard_map/all_gather | solution.py:67
  258.8 2.4 copy-start.1
  260.8 1.7 copy-start.6
  260.9 1.7 copy-start.7
  262.6 1.7 copy-start.8
  262.6 16.4 %copy-start.9 = (s32[2]{0:T(128)S(1)}, s32[2]{0:T(128)}, u32[]{:S(2)}) copy-start(s32[2]{0:T(128)} %param.19) | copy-start | bytes 28
Sparse Core Ops, SparseCore 0:
  54.3 38.3 reduce-scatter.3
  97.9 160.8 all-reduce.2
  264.3 60.1 all-gather.2
